TPU v7x, 128 devices: a whole 4x4x4 slice. The times are simulated.
128 devices in a mesh: sec: 2 (over core), tile: 64 (over y, x, z).
Axes of the slice: x: 4, y: 4, z: 4, core: 2. Of those that a mesh axis runs over, the one named last changes fastest.
Arguments:
- section_state: float32 [2, 72, 1048576], P('sec', None, 'tile'), may hold values from -6 to 6
- matrices: float32 [2, 72, 72], replicated, may hold values from -0.75 to 0.75
- blocks: bfloat16 [2, 16384, 128, 128], P('sec', 'tile'), may hold values from -0.5 to 0.5
- src_slot: int32 [2, 16384], P('sec', 'tile'), may hold values from 0 to 127
- dst_dev: int32 [2, 16384, 1], P('sec', 'tile'), may hold values from 0 to 63; in each aligned block of 256 rows (0 to 255, 256 to 511, ..., all dimensions but the last counted through in order) at most 8 rows name the same one
- dst_slot: int32 [2, 16384], P('sec', 'tile'), may hold values from 0 to 127
Outputs:
- new_state: float32 [2, 72, 1048576], P('sec', None, 'tile')
Inputs may be any that keep to these rules, and one draw needn't show every extreme that they name: `dst_dev`: in the rows of one device (aligned blocks of 256 rows along the second dimension), no destination index occurs more than 8 times, and some index occurs exactly 8 times.
All inputs are finite; a program needn't handle non-finite values.
Results may differ from a plain program's by a relative error of at most 0.0015.
Values sent between devices are 32-bit elements; how exact they have to be, the bound alone decides.
A program may use at most 128 MiB of HBM per device.

v0:
```python
import functools
import itertools
import random

import jax
import jax.numpy as jnp
from jax import lax
from jax.experimental import pallas as pl
from jax.experimental.pallas import tpu as pltpu
from jax.sharding import PartitionSpec as P

MESH = pl.DeviceIdType.MESH
FIELDS = 8
DEPTH = 8
LANES = 128
STEPS = 4
ATMOS_VISC = 0.22
OCEAN_VISC = 0.24


def torus(count):
    side = round(count ** (1 / 3))
    return (side, side, side)


def send_order(dims):
    offsets = list(itertools.product(*[range(n) for n in dims]))
    random.Random(1).shuffle(offsets)

    def hops(offset):
        return sum(min(a, n - a) for a, n in zip(offset, dims))

    return sorted(offsets, key=lambda offset: -hops(offset))


def split(value):
    high = value.astype(jnp.bfloat16).astype(jnp.float32)
    return high, value - high


def stacked(value):
    high, low = split(value)
    return jnp.concatenate([high, low, high], axis=0).astype(jnp.bfloat16)


def weights(matrix):
    high, low = split(matrix)
    return jnp.concatenate([high, high, low], axis=1).astype(jnp.bfloat16)


def column(row):
    return jnp.transpose(jnp.broadcast_to(row, (8, row.shape[1])))[:, :1]


def exchange(
    dims,
    state_hbm,
    mats,
    blocks_hbm,
    src_slot,
    dst_dev,
    dst_slot,
    out_hbm,
    north_hbm,
    south_hbm,
    blocks_v,
    export_v,
    cells_v,
    part_v,
    out_v,
    recv_v,
    meta_v,
    meta_r,
    x_v,
    p_v,
    imp_v,
    place_v,
    place_s,
    load_sem,
    place_sem,
    send_sem,
    recv_sem,
    msend_sem,
    mrecv_sem,
    hsend_sem,
    hrecv_sem,
    store_sem,
):
    levels, cells = x_v.shape
    tiles = cells // LANES
    blocks = blocks_v.shape[0]
    peers = dims[0] * dims[1] * dims[2]
    order = send_order(dims)
    section = lax.axis_index("sec")
    me = lax.axis_index("tile")
    other = 1 - section
    y, x, z = me // (dims[1] * dims[2]), (me // dims[2]) % dims[1], me % dims[2]

    def at(offset, sign):
        dy, dx, dz = offset
        ny, nx, nz = dims
        return (
            ((y + ny + sign * dy) % ny) * (nx * nz)
            + ((x + nx + sign * dx) % nx) * nz
            + (z + nz + sign * dz) % nz
        )

    after, before = (me + 1) % peers, (me + peers - 1) % peers

    start = other * (levels - FIELDS)
    get_export = pltpu.make_async_copy(state_hbm.at[pl.ds(start, FIELDS)], export_v, load_sem.at[0])
    get_export.start()
    chunks = 8
    per = blocks // chunks
    get_blocks = []
    for c in range(chunks):
        get = pltpu.make_async_copy(
            blocks_hbm.at[pl.ds(c * per, per)], blocks_v.at[pl.ds(c * per, per)], load_sem.at[1 + c]
        )
        get.start()
        get_blocks.append(get)
    get_state = pltpu.make_async_copy(state_hbm, x_v, load_sem.at[1 + chunks])
    get_state.start()

    barrier = pltpu.get_barrier_semaphore()
    for offset in order:
        pl.semaphore_signal(barrier, inc=1, device_id=(other, at(offset, -1)), device_id_type=MESH)
    for side in (before, after):
        pl.semaphore_signal(barrier, inc=1, device_id=(section, side), device_id_type=MESH)

    owner = dst_dev[...]
    earlier = lax.broadcasted_iota(jnp.int32, (blocks, blocks), 0) < lax.broadcasted_iota(
        jnp.int32, (blocks, blocks), 1
    )
    alike = earlier & (column(owner) == owner)
    position = owner * DEPTH + jnp.sum(jnp.where(alike, 1, 0), axis=0, keepdims=True)
    fills = column(position) == lax.broadcasted_iota(jnp.int32, (blocks, peers * DEPTH), 1)
    number = lax.broadcasted_iota(jnp.int32, (blocks, peers * DEPTH), 0)
    place_v[0:1, :] = jnp.sum(jnp.where(fills, number, 0), axis=0, keepdims=True)
    place_v[1:2, :] = jnp.sum(jnp.where(fills, column(dst_slot[...]) + 1, 0), axis=0, keepdims=True)
    get_place = pltpu.make_async_copy(place_v, place_s, place_sem)
    get_place.start()

    get_export.wait()
    for tile in range(tiles):
        cells_v[tile] = export_v[:, tile * LANES : (tile + 1) * LANES]
    for c in range(chunks):
        get_blocks[c].wait()

        def remap(i, carry, c=c):
            for u in range(8):
                b = c * per + i * 8 + u
                tile = src_slot[0, b]
                part_v[b] = lax.dot_general(
                    cells_v[tile].astype(jnp.bfloat16),
                    blocks_v[b],
                    (((1,), (1,)), ((), ())),
                    preferred_element_type=jnp.float32,
                )
            return carry

        lax.fori_loop(0, per // 8, remap, 0)

    get_place.wait()
    pl.semaphore_wait(barrier, peers + 2)

    rows = DEPTH * FIELDS
    lane = lax.broadcasted_iota(jnp.int32, (1, LANES), 1)
    group = LANES // DEPTH
    data, meta = [], []
    for k, offset in enumerate(order):
        dest = at(offset, 1)
        line = jnp.zeros((1, LANES), jnp.int32)
        for r in range(DEPTH):
            b = place_s[0, dest * DEPTH + r]
            out_v[pl.ds(k * rows + r * FIELDS, FIELDS), :] = part_v[b]
            line = jnp.where(lane == (k % group) * DEPTH + r, place_s[1, dest * DEPTH + r], line)
        meta_v[k] = line.astype(jnp.float32)
        target = (other, dest)
        copy = pltpu.make_async_remote_copy(
            src_ref=out_v.at[pl.ds(k * rows, rows)],
            dst_ref=recv_v.at[pl.ds(k * rows, rows)],
            send_sem=send_sem.at[k],
            recv_sem=recv_sem.at[k],
            device_id=target,
            device_id_type=MESH,
        )
        copy.start()
        data.append(copy)
        copy = pltpu.make_async_remote_copy(
            src_ref=meta_v.at[k],
            dst_ref=meta_r.at[k],
            send_sem=msend_sem.at[k],
            recv_sem=mrecv_sem.at[k],
            device_id=target,
            device_id_type=MESH,
        )
        copy.start()
        meta.append(copy)

    matrix = mats[section]
    full = weights(matrix)
    edge = weights(jnp.where(section == 0, matrix[:, levels - FIELDS :], matrix[:, :FIELDS]))
    width = 512
    get_state.wait()

    def ahead(i, carry):
        cols = pl.ds(pl.multiple_of(i * width, width), width)
        p_v[:, cols] = jnp.dot(full, stacked(x_v[:, cols]), preferred_element_type=jnp.float32)
        return carry

    lax.fori_loop(0, cells // width, ahead, 0)

    tile_number = lax.broadcasted_iota(jnp.int32, (tiles, LANES), 0).astype(jnp.float32)
    for q in range(peers // group):
        line = jnp.zeros((1, LANES), jnp.float32)
        for k in range(q * group, (q + 1) * group):
            meta[k].wait_recv()
            line = line + meta_r[k]
            data[k].wait_recv()
        chosen = (tile_number == line - 1.0).astype(jnp.float32)
        chosen = jnp.concatenate([chosen, chosen], axis=1).astype(jnp.bfloat16)
        for f in range(FIELDS):
            value = recv_v[pl.ds(q * group * rows + f, group * DEPTH, stride=FIELDS), :]
            high, low = split(value)
            term = jnp.dot(
                chosen,
                jnp.concatenate([high, low], axis=0).astype(jnp.bfloat16),
                preferred_element_type=jnp.float32,
            )
            to = pl.ds(f, tiles, stride=FIELDS)
            if q == 0:
                imp_v[to, :] = term
            else:
                imp_v[to, :] = imp_v[to, :] + term

    per_width = width // LANES

    def columns(i, substeps):
        cols = pl.ds(pl.multiple_of(i * width, width), width)
        imported = jnp.concatenate(
            [
                imp_v[pl.ds(pl.multiple_of((i * per_width + j) * FIELDS, FIELDS), FIELDS), :]
                for j in range(per_width)
            ],
            axis=1,
        )
        x_v[pl.ds(start, FIELDS), cols] = x_v[pl.ds(start, FIELDS), cols] + imported
        product = p_v[:, cols] + jnp.dot(edge, stacked(imported), preferred_element_type=jnp.float32)
        value = x_v[:, cols] + 0.5 * jnp.tanh(product)
        if substeps == 2:
            product = jnp.dot(full, stacked(value), preferred_element_type=jnp.float32)
            value = value + 0.5 * jnp.tanh(product)
        x_v[:, cols] = value

    halo = STEPS * LANES
    last = cells // width - 1

    def both(i):
        @pl.when(section == 0)
        def _():
            columns(i, 2)

        @pl.when(section == 1)
        def _():
            columns(i, 1)

    both(0)
    both(last)
    to_before = pltpu.make_async_remote_copy(
        src_ref=x_v.at[:, pl.ds(0, halo)],
        dst_ref=south_hbm,
        send_sem=hsend_sem.at[0],
        recv_sem=hrecv_sem.at[0],
        device_id=(section, before),
        device_id_type=MESH,
    )
    to_after = pltpu.make_async_remote_copy(
        src_ref=x_v.at[:, pl.ds(cells - halo, halo)],
        dst_ref=north_hbm,
        send_sem=hsend_sem.at[1],
        recv_sem=hrecv_sem.at[1],
        device_id=(section, after),
        device_id_type=MESH,
    )
    to_before.start()
    to_after.start()
    pieces = 4
    span = cells // pieces
    stores = []
    for piece in range(pieces):
        low = max(1, piece * span // width)
        high = min(last, (piece + 1) * span // width)

        @pl.when(section == 0)
        def _(low=low, high=high):
            lax.fori_loop(low, high, lambda i, carry: (columns(i, 2), carry)[1], 0)

        @pl.when(section == 1)
        def _(low=low, high=high):
            lax.fori_loop(low, high, lambda i, carry: (columns(i, 1), carry)[1], 0)

        store = pltpu.make_async_copy(
            x_v.at[:, pl.ds(piece * span, span)], out_hbm.at[:, pl.ds(piece * span, span)], store_sem.at[piece]
        )
        store.start()
        stores.append(store)
    for copy in data + meta:
        copy.wait_send()
    for store in stores:
        store.wait()
    for copy in (to_before, to_after):
        copy.wait()


def diffuse(x_ref, north_ref, south_ref, o_ref):
    levels, cells = x_ref.shape
    rows = cells // LANES
    streams = levels // 8
    section = lax.axis_index("sec")
    me = lax.axis_index("tile")
    peers = lax.axis_size("tile")
    visc = jnp.where(section == 0, ATMOS_VISC, OCEAN_VISC).astype(jnp.float32)
    center = (1.0 - 4.0 * visc) / visc
    scale = (visc * visc) * (visc * visc)
    top = jnp.where(me == 0, 0.0, 1.0).astype(jnp.float32)
    bottom = jnp.where(me == peers - 1, 0.0, 1.0).astype(jnp.float32)

    def advance(new, carry, masks):
        out = []
        for s in range(streams):
            value = new[s]
            kept = []
            for k in range(STEPS):
                part, prior = carry[s][k]
                if masks[k] is not None:
                    value = value * masks[k]
                fresh = (
                    center * value
                    + (pltpu.roll(value, 1, 1) + pltpu.roll(value, LANES - 1, 1))
                    + prior
                )
                kept.append((fresh, value))
                value = part + value
            out.append((value, tuple(kept)))
        return [v for v, _ in out], tuple(k for _, k in out)

    zero = jnp.zeros((8, LANES), jnp.float32)
    carry = tuple(tuple((zero, zero) for _ in range(STEPS)) for _ in range(streams))

    def load(ref, row):
        at = row * LANES if isinstance(row, int) else pl.multiple_of(row * LANES, LANES)
        return [ref[pl.ds(8 * s, 8), pl.ds(at, LANES)] for s in range(streams)]

    def store(row, values):
        at = row * LANES if isinstance(row, int) else pl.multiple_of(row * LANES, LANES)
        for s in range(streams):
            o_ref[0, pl.ds(8 * s, 8), pl.ds(at, LANES)] = values[s] * scale

    def masks_at(row):
        return [top if row - k < 0 else (bottom if row - k >= rows else None) for k in range(STEPS)]

    for row in range(-STEPS, STEPS):
        new = load(north_ref, row + STEPS) if row < 0 else load(x_ref, row)
        _, carry = advance(new, carry, masks_at(row))

    unroll = 4

    def body(i, carry):
        for u in range(unroll):
            row = STEPS + i * unroll + u
            values, carry = advance(load(x_ref, row), carry, [None] * STEPS)
            store(row - STEPS, values)
        return carry

    carry = lax.fori_loop(0, (rows - STEPS) // unroll, body, carry)
    for row in range(rows, rows + STEPS):
        values, carry = advance(load(south_ref, row - rows), carry, masks_at(row))
        store(row - STEPS, values)


def per_device(dims, section_state, matrices, blocks, src_slot, dst_dev, dst_slot):
    _, levels, cells = section_state.shape
    block_count = blocks.shape[1]
    tiles = cells // LANES
    peers = dims[0] * dims[1] * dims[2]
    halo = STEPS * LANES
    f32, i32, dma = jnp.float32, jnp.int32, pltpu.SemaphoreType.DMA
    anywhere = pl.BlockSpec(memory_space=pl.ANY)
    vmem = pl.BlockSpec(memory_space=pltpu.VMEM)
    slots = peers * DEPTH * FIELDS
    state, north, south = pl.pallas_call(
        functools.partial(exchange, dims),
        out_shape=[
            jax.ShapeDtypeStruct((levels, cells), f32),
            jax.ShapeDtypeStruct((levels, halo), f32),
            jax.ShapeDtypeStruct((levels, halo), f32),
        ],
        in_specs=[anywhere, vmem, anywhere, pl.BlockSpec(memory_space=pltpu.SMEM), vmem, vmem],
        out_specs=[anywhere, anywhere, anywhere],
        scratch_shapes=[
            pltpu.VMEM((block_count, LANES, LANES), jnp.bfloat16),
            pltpu.VMEM((FIELDS, cells), f32),
            pltpu.VMEM((tiles, FIELDS, LANES), f32),
            pltpu.VMEM((block_count, FIELDS, LANES), f32),
            pltpu.VMEM((slots, LANES), f32),
            pltpu.VMEM((slots, LANES), f32),
            pltpu.VMEM((peers, 1, LANES), f32),
            pltpu.VMEM((peers, 1, LANES), f32),
            pltpu.VMEM((levels, cells), f32),
            pltpu.VMEM((levels, cells), f32),
            pltpu.VMEM((tiles * FIELDS, LANES), f32),
            pltpu.VMEM((8, peers * DEPTH), i32),
            pltpu.SMEM((8, peers * DEPTH), i32),
            dma((10,)),
            dma,
            dma((peers,)),
            dma((peers,)),
            dma((peers,)),
            dma((peers,)),
            dma((2,)),
            dma((2,)),
            dma((4,)),
        ],
        compiler_params=pltpu.CompilerParams(
            collective_id=0, has_side_effects=True, vmem_limit_bytes=48 << 20
        ),
    )(
        section_state.reshape(levels, cells),
        matrices,
        blocks.reshape(block_count, LANES, LANES),
        src_slot,
        dst_dev.reshape(1, block_count),
        dst_slot,
    )
    band = 24
    return pl.pallas_call(
        diffuse,
        grid=(levels // band,),
        out_shape=jax.ShapeDtypeStruct((1, levels, cells), f32),
        in_specs=[
            pl.BlockSpec((band, cells), lambda i: (i, 0)),
            pl.BlockSpec((band, halo), lambda i: (i, 0)),
            pl.BlockSpec((band, halo), lambda i: (i, 0)),
        ],
        out_specs=pl.BlockSpec((1, band, cells), lambda i: (0, i, 0)),
        compiler_params=pltpu.CompilerParams(vmem_limit_bytes=32 << 20),
    )(state, north, south)


def solution(mesh):
    in_specs = (
        P("sec", None, "tile"),
        P(),
        P("sec", "tile", None, None),
        P("sec", "tile"),
        P("sec", "tile", None),
        P("sec", "tile"),
    )
    return jax.shard_map(
        functools.partial(per_device, torus(mesh.shape["tile"])),
        mesh=mesh,
        in_specs=in_specs,
        out_specs=P("sec", None, "tile"),
        check_vma=False,
    )
```

profile of v0, /device:TPU:0, one launch (start us, length us, event | category | flops | bytes accessed | tf_op | source)
XLA Modules:
  0.0 86.8 jit_solution(16820680774664776217)
XLA Ops:
  0.0 0.0 copy-start
  0.0 0.9 %copy-done = f32[2,72,72]{2,1,0:T(8,128)S(1)} copy-done((f32[2,72,72]{2,1,0:T(8,128)S(1)}, f32[2,72,72]{2,1,0:T(8,128)}, u32[]{:S(2)}) %copy-start) | copy-done | bytes 41496
  0.9 0.0 copy-start.1
  0.9 0.7 copy-done.1
  1.6 0.0 copy-start.2
  1.6 0.7 copy-done.2
  2.2 0.0 copy-start.3
  2.2 0.7 copy-done.3
  2.9 53.7 %shard_map.64 = (f32[72,16384]{1,0:T(8,128)S(1)}, f32[72,512]{1,0:T(8,128)S(1)}, f32[72,512]{1,0:T(8,128)S(1)}) custom-call(f32[72,16384]{1,0:T(8,128)} %bitcast.5, f32[2,72,72]{2,1,0:T(8,128)S(1)} %copy-done, bf16[256,128,128]{2,1,0:T(8,128)(2,1)} %bitcast.4, s32[1,256]{1,0:T(1,128)S(1)} %copy-done.1, s32[1,256]{1,0:T(1,128)S(1)} %bitcast.3, ...), custom_call_target="tpu_custom_call" | custom-call | tf_op jit(solution)/shard_map/pallas_call | solution.py:392
  56.6 30.2 %shard_map.65 = f32[1,72,16384]{2,1,0:T(8,128)} custom-call(f32[72,16384]{1,0:T(8,128)S(1)} %get-tuple-element.8.x_ref, f32[72,512]{1,0:T(8,128)S(1)} %get-tuple-element.9.north_ref, f32[72,512]{1,0:T(8,128)S(1)} %get-tuple-element.10.south_ref), custom_call_target="tpu_custom_call" | custom-call | tf_op jit(solution)/shard_map/pallas_call | solution.py:437
Async XLA Ops:
  0.0 0.9 %copy-start = (f32[2,72,72]{2,1,0:T(8,128)S(1)}, f32[2,72,72]{2,1,0:T(8,128)}, u32[]{:S(2)}) copy-start(f32[2,72,72]{2,1,0:T(8,128)} %mats.1) | copy-start | bytes 124420
  0.9 0.7 copy-start.1
  1.6 0.7 copy-start.2
  2.2 0.7 copy-start.3
where the time goes:
time: 87.7 us; the launch traced here: 86.8 us
  Pallas kernels  83.9 us (96%)
  local copies, waits for them, and re-layouts  2.92 us (3%)
    pallas_call x1, Pallas kernels, per_device(): pl.pallas_call(functools.partial(exchange, dims), out_shape=[jax.ShapeDty...  53.7 us
    pallas_call x1, Pallas kernels, per_device(): pl.pallas_call(diffuse, grid=(levels // band,), out_shape=jax.ShapeDtypeS...  30.2 us
    unnamed x8, local copies, waits for them, and re-layouts  2.92 us

commit v1 on v0

--- a/solution.py
+++ b/solution.py
@@ -16,6 +16,7 @@
 STEPS = 4
 ATMOS_VISC = 0.22
 OCEAN_VISC = 0.24
+VMEM_BYTES = 60 << 20
 
 
 def torus(count):
@@ -112,15 +113,13 @@
     get_export.start()
     chunks = 8
     per = blocks // chunks
-    get_blocks = []
+
+    def get_blocks(c):
+        part = pl.ds(c * per, per)
+        return pltpu.make_async_copy(blocks_hbm.at[part], blocks_v.at[part], load_sem.at[1 + c])
+
     for c in range(chunks):
-        get = pltpu.make_async_copy(
-            blocks_hbm.at[pl.ds(c * per, per)], blocks_v.at[pl.ds(c * per, per)], load_sem.at[1 + c]
-        )
-        get.start()
-        get_blocks.append(get)
-    get_state = pltpu.make_async_copy(state_hbm, x_v, load_sem.at[1 + chunks])
-    get_state.start()
+        get_blocks(c).start()
 
     barrier = pltpu.get_barrier_semaphore()
     for offset in order:
@@ -144,23 +143,25 @@
     get_export.wait()
     for tile in range(tiles):
         cells_v[tile] = export_v[:, tile * LANES : (tile + 1) * LANES]
-    for c in range(chunks):
-        get_blocks[c].wait()
-
-        def remap(i, carry, c=c):
-            for u in range(8):
-                b = c * per + i * 8 + u
-                tile = src_slot[0, b]
-                part_v[b] = lax.dot_general(
-                    cells_v[tile].astype(jnp.bfloat16),
-                    blocks_v[b],
-                    (((1,), (1,)), ((), ())),
-                    preferred_element_type=jnp.float32,
-                )
-            return carry
-
-        lax.fori_loop(0, per // 8, remap, 0)
-
+
+    def remap(c, carry):
+        get_blocks(c).wait()
+        for u in range(0, per, 2):
+            b = c * per + u
+            cell = jnp.concatenate([cells_v[src_slot[0, b]], cells_v[src_slot[0, b + 1]]], axis=0)
+            both = lax.dot_general(
+                cell.astype(jnp.bfloat16),
+                blocks_v[pl.ds(b, 2)].reshape(2 * LANES, LANES),
+                (((1,), (1,)), ((), ())),
+                preferred_element_type=jnp.float32,
+            )
+            part_v[b] = both[:FIELDS, :LANES]
+            part_v[b + 1] = both[FIELDS:, LANES:]
+        return carry
+
+    lax.fori_loop(0, chunks, remap, 0)
+    get_state = pltpu.make_async_copy(state_hbm, x_v, load_sem.at[1 + chunks])
+    get_state.start()
     get_place.wait()
     pl.semaphore_wait(barrier, peers + 2)
 
@@ -234,9 +235,16 @@
             else:
                 imp_v[to, :] = imp_v[to, :] + term
 
+    width = 2048
+    chunks = cells // width
     per_width = width // LANES
 
-    def columns(i, substeps):
+    def put(i):
+        cols = pl.ds(pl.multiple_of(i * width, width), width)
+        return pltpu.make_async_copy(x_v.at[:, cols], out_hbm.at[:, cols], store_sem.at[i])
+
+    def columns(substeps, i, carry):
+        i = (i + chunks - 1) % chunks
         cols = pl.ds(pl.multiple_of(i * width, width), width)
         imported = jnp.concatenate(
             [
@@ -252,21 +260,18 @@
             product = jnp.dot(full, stacked(value), preferred_element_type=jnp.float32)
             value = value + 0.5 * jnp.tanh(product)
         x_v[:, cols] = value
-
+        put(i).start()
+        return carry
+
+    def physics(low, high):
+        for number in range(2):
+
+            @pl.when(section == number)
+            def _(number=number):
+                lax.fori_loop(low, high, functools.partial(columns, 2 - number), 0)
+
+    physics(0, 2)
     halo = STEPS * LANES
-    last = cells // width - 1
-
-    def both(i):
-        @pl.when(section == 0)
-        def _():
-            columns(i, 2)
-
-        @pl.when(section == 1)
-        def _():
-            columns(i, 1)
-
-    both(0)
-    both(last)
     to_before = pltpu.make_async_remote_copy(
         src_ref=x_v.at[:, pl.ds(0, halo)],
         dst_ref=south_hbm,
@@ -285,38 +290,36 @@
     )
     to_before.start()
     to_after.start()
-    pieces = 4
-    span = cells // pieces
-    stores = []
-    for piece in range(pieces):
-        low = max(1, piece * span // width)
-        high = min(last, (piece + 1) * span // width)
-
-        @pl.when(section == 0)
-        def _(low=low, high=high):
-            lax.fori_loop(low, high, lambda i, carry: (columns(i, 2), carry)[1], 0)
-
-        @pl.when(section == 1)
-        def _(low=low, high=high):
-            lax.fori_loop(low, high, lambda i, carry: (columns(i, 1), carry)[1], 0)
-
-        store = pltpu.make_async_copy(
-            x_v.at[:, pl.ds(piece * span, span)], out_hbm.at[:, pl.ds(piece * span, span)], store_sem.at[piece]
-        )
-        store.start()
-        stores.append(store)
+    physics(2, chunks)
     for copy in data + meta:
         copy.wait_send()
-    for store in stores:
-        store.wait()
+    for i in range(chunks):
+        put(i).wait()
     for copy in (to_before, to_after):
         copy.wait()
 
 
-def diffuse(x_ref, north_ref, south_ref, o_ref):
+def ring_powers():
+    shape = (2 * LANES, LANES)
+    apart = (
+        lax.broadcasted_iota(jnp.int32, shape, 0) + 2 * LANES - lax.broadcasted_iota(jnp.int32, shape, 1)
+    ) % LANES
+    terms = []
+    for entries in ({1: 4}, {0: 12, 2: 6}, {1: 12, 3: 4}, {0: 6, 2: 4, 4: 1}):
+        term = jnp.zeros(shape, jnp.float32)
+        for distance, weight in entries.items():
+            near = (apart == distance) | (apart == (LANES - distance) % LANES)
+            term = jnp.where(near, float(weight), term)
+        terms.append(term.astype(jnp.bfloat16))
+    return jnp.concatenate(terms, axis=1)
+
+
+def diffuse(x_ref, north_ref, south_ref, o_ref, coef_ref, side_ref):
     levels, cells = x_ref.shape
     rows = cells // LANES
     streams = levels // 8
+    chunk = 32
+    first = 2 * STEPS
     section = lax.axis_index("sec")
     me = lax.axis_index("tile")
     peers = lax.axis_size("tile")
@@ -326,56 +329,84 @@
     top = jnp.where(me == 0, 0.0, 1.0).astype(jnp.float32)
     bottom = jnp.where(me == peers - 1, 0.0, 1.0).astype(jnp.float32)
 
-    def advance(new, carry, masks):
-        out = []
+    @pl.when(pl.program_id(0) == 0)
+    def _():
+        coef_ref[...] = ring_powers()
+
+    coef = coef_ref[...]
+
+    def at(row):
+        return row * LANES if isinstance(row, int) else pl.multiple_of(row * LANES, LANES)
+
+    def load(ref, row):
+        return [ref[pl.ds(8 * s, 8), pl.ds(at(row), LANES)] for s in range(streams)]
+
+    def store(row, values):
         for s in range(streams):
-            value = new[s]
-            kept = []
+            o_ref[0, pl.ds(8 * s, 8), pl.ds(at(row), LANES)] = values[s] * scale
+
+    def sides(ref, row, count, place):
+        value = jnp.concatenate([v for i in range(count) for v in load(ref, row + i)], axis=0)
+        high = value.astype(jnp.bfloat16)
+        low = (value - high.astype(jnp.float32)).astype(jnp.bfloat16)
+        terms = jnp.dot(
+            jnp.concatenate([high, low], axis=1), coef, preferred_element_type=jnp.float32
+        )
+        for i in range(count):
+            for s in range(streams):
+                m = (i * streams + s) * 8
+                for k in range(STEPS):
+                    side_ref[place + i, s, k] = terms[m : m + 8, k * LANES : (k + 1) * LANES]
+
+    def advance(new, carry, row, edges):
+        values, kept = [], []
+        for s in range(streams):
+            value, parts = new[s], []
             for k in range(STEPS):
                 part, prior = carry[s][k]
-                if masks[k] is not None:
-                    value = value * masks[k]
-                fresh = (
-                    center * value
-                    + (pltpu.roll(value, 1, 1) + pltpu.roll(value, LANES - 1, 1))
-                    + prior
-                )
-                kept.append((fresh, value))
+                if edges and row - k < 0:
+                    value = value * top
+                if edges and row - k >= rows:
+                    value = value * bottom
+                parts.append((center * value + (side_ref[first + row - k, s, k] + prior), value))
                 value = part + value
-            out.append((value, tuple(kept)))
-        return [v for v, _ in out], tuple(k for _, k in out)
+            values.append(value)
+            kept.append(tuple(parts))
+        return values, tuple(kept)
 
     zero = jnp.zeros((8, LANES), jnp.float32)
     carry = tuple(tuple((zero, zero) for _ in range(STEPS)) for _ in range(streams))
-
-    def load(ref, row):
-        at = row * LANES if isinstance(row, int) else pl.multiple_of(row * LANES, LANES)
-        return [ref[pl.ds(8 * s, 8), pl.ds(at, LANES)] for s in range(streams)]
-
-    def store(row, values):
-        at = row * LANES if isinstance(row, int) else pl.multiple_of(row * LANES, LANES)
+    for row in range(STEPS):
         for s in range(streams):
-            o_ref[0, pl.ds(8 * s, 8), pl.ds(at, LANES)] = values[s] * scale
-
-    def masks_at(row):
-        return [top if row - k < 0 else (bottom if row - k >= rows else None) for k in range(STEPS)]
-
-    for row in range(-STEPS, STEPS):
-        new = load(north_ref, row + STEPS) if row < 0 else load(x_ref, row)
-        _, carry = advance(new, carry, masks_at(row))
-
-    unroll = 4
-
-    def body(i, carry):
-        for u in range(unroll):
-            row = STEPS + i * unroll + u
-            values, carry = advance(load(x_ref, row), carry, [None] * STEPS)
+            for k in range(STEPS):
+                side_ref[row, s, k] = zero
+    sides(north_ref, 0, STEPS, first - STEPS)
+    sides(x_ref, 0, chunk, first)
+    for row in range(-STEPS, 0):
+        _, carry = advance(load(north_ref, row + STEPS), carry, row, True)
+
+    def several(i, carry, start=0, edges=False):
+        for u in range(start, chunk):
+            row = i * chunk + u
+            values, carry = advance(load(x_ref, row), carry, row, edges)
             store(row - STEPS, values)
         return carry
 
-    carry = lax.fori_loop(0, (rows - STEPS) // unroll, body, carry)
+    for row in range(STEPS):
+        _, carry = advance(load(x_ref, row), carry, row, True)
+    sides(x_ref, chunk, chunk, first + chunk)
+    carry = several(0, carry, STEPS)
+
+    def body(i, carry):
+        sides(x_ref, (i + 1) * chunk, chunk, first + (i + 1) * chunk)
+        return several(i, carry)
+
+    last = rows // chunk - 1
+    carry = lax.fori_loop(1, last, body, carry)
+    sides(south_ref, 0, STEPS, first + rows)
+    carry = several(last, carry)
     for row in range(rows, rows + STEPS):
-        values, carry = advance(load(south_ref, row - rows), carry, masks_at(row))
+        values, carry = advance(load(south_ref, row - rows), carry, row, True)
         store(row - STEPS, values)
 
 
@@ -420,10 +451,10 @@
             dma((peers,)),
             dma((2,)),
             dma((2,)),
-            dma((4,)),
+            dma((8,)),
         ],
         compiler_params=pltpu.CompilerParams(
-            collective_id=0, has_side_effects=True, vmem_limit_bytes=48 << 20
+            collective_id=0, has_side_effects=True, vmem_limit_bytes=VMEM_BYTES
         ),
     )(
         section_state.reshape(levels, cells),
@@ -444,7 +475,11 @@
             pl.BlockSpec((band, halo), lambda i: (i, 0)),
         ],
         out_specs=pl.BlockSpec((1, band, cells), lambda i: (0, i, 0)),
-        compiler_params=pltpu.CompilerParams(vmem_limit_bytes=32 << 20),
+        scratch_shapes=[
+            pltpu.VMEM((2 * LANES, STEPS * LANES), jnp.bfloat16),
+            pltpu.VMEM((cells // LANES + 3 * STEPS, band // 8, STEPS, 8, LANES), f32),
+        ],
+        compiler_params=pltpu.CompilerParams(vmem_limit_bytes=VMEM_BYTES),
     )(state, north, south)
 
 

time: 87.7 us -> 58.4 us (0.67)
  Pallas kernels: 83.9 us -> 58.2 us
  local copies, waits for them, and re-layouts: 2.92 us -> 0 us
    pallas_call x1, Pallas kernels: 30.2 us -> 9.32 us  [per_device(): pl.pallas_call(diffuse, grid=(levels // band,), out_shape=jax.ShapeDtypeS...]
    pallas_call x1, Pallas kernels: 53.7 us -> 48.9 us  [per_device(): pl.pallas_call(functools.partial(exchange, dims), out_shape=[jax.ShapeDty...]
    unnamed x8 -> x0, local copies, waits for them, and re-layouts: 2.92 us -> none
where the time goes in v1:
time: 58.4 us; the launch traced here: 58.2 us
  Pallas kernels  58.2 us (100%)
    pallas_call x1, Pallas kernels, per_device(): pl.pallas_call(functools.partial(exchange, dims), out_shape=[jax.ShapeDty...  48.9 us
    pallas_call x1, Pallas kernels, per_device(): pl.pallas_call(diffuse, grid=(levels // band,), out_shape=jax.ShapeDtypeS...  9.32 us

profile of v1, /device:TPU:0, one launch (start us, length us, event | category | flops | bytes accessed | tf_op | source)
XLA Modules:
  0.0 58.2 jit_solution(4187135071655673119)
XLA Ops:
  0.0 48.9 %shard_map.64 = (f32[72,16384]{1,0:T(8,128)}, f32[72,512]{1,0:T(8,128)}, f32[72,512]{1,0:T(8,128)}) custom-call(f32[72,16384]{1,0:T(8,128)} %bitcast.4, f32[2,72,72]{2,1,0:T(8,128)} %mats.1, bf16[256,128,128]{2,1,0:T(8,128)(2,1)} %bitcast.3, s32[1,256]{1,0:T(1,128)} %src_slot.1, s32[1,256]{1,0:T(1,128)} %bitcast.5, s32[1,256]{1,0:T(1,128)} %dst_slot.1), custom_call_target="tpu_custom_call" | custom-call | tf_op jit(solution)/shard_map/pallas_call | solution.py:423
  48.9 9.3 %shard_map.65 = f32[1,72,16384]{2,1,0:T(8,128)} custom-call(f32[72,16384]{1,0:T(8,128)} %get-tuple-element.8.x_ref, f32[72,512]{1,0:T(8,128)} %get-tuple-element.9.north_ref, f32[72,512]{1,0:T(8,128)} %get-tuple-element.10.south_ref), custom_call_target="tpu_custom_call" | custom-call | tf_op jit(solution)/shard_map/pallas_call | solution.py:468

commit v2 on v1

--- a/solution.py
+++ b/solution.py
@@ -14,6 +14,7 @@
 DEPTH = 8
 LANES = 128
 STEPS = 4
+HALF = 2
 ATMOS_VISC = 0.22
 OCEAN_VISC = 0.24
 VMEM_BYTES = 60 << 20
@@ -62,8 +63,6 @@
     dst_dev,
     dst_slot,
     out_hbm,
-    north_hbm,
-    south_hbm,
     blocks_v,
     export_v,
     cells_v,
@@ -75,6 +74,9 @@
     x_v,
     p_v,
     imp_v,
+    north_v,
+    south_v,
+    coef_v,
     place_v,
     place_s,
     load_sem,
@@ -198,6 +200,8 @@
         )
         copy.start()
         meta.append(copy)
+
+    coef_v[...] = ring_powers()
 
     matrix = mats[section]
     full = weights(matrix)
@@ -239,10 +243,6 @@
     chunks = cells // width
     per_width = width // LANES
 
-    def put(i):
-        cols = pl.ds(pl.multiple_of(i * width, width), width)
-        return pltpu.make_async_copy(x_v.at[:, cols], out_hbm.at[:, cols], store_sem.at[i])
-
     def columns(substeps, i, carry):
         i = (i + chunks - 1) % chunks
         cols = pl.ds(pl.multiple_of(i * width, width), width)
@@ -260,7 +260,6 @@
             product = jnp.dot(full, stacked(value), preferred_element_type=jnp.float32)
             value = value + 0.5 * jnp.tanh(product)
         x_v[:, cols] = value
-        put(i).start()
         return carry
 
     def physics(low, high):
@@ -274,7 +273,7 @@
     halo = STEPS * LANES
     to_before = pltpu.make_async_remote_copy(
         src_ref=x_v.at[:, pl.ds(0, halo)],
-        dst_ref=south_hbm,
+        dst_ref=south_v,
         send_sem=hsend_sem.at[0],
         recv_sem=hrecv_sem.at[0],
         device_id=(section, before),
@@ -282,7 +281,7 @@
     )
     to_after = pltpu.make_async_remote_copy(
         src_ref=x_v.at[:, pl.ds(cells - halo, halo)],
-        dst_ref=north_hbm,
+        dst_ref=north_v,
         send_sem=hsend_sem.at[1],
         recv_sem=hrecv_sem.at[1],
         device_id=(section, after),
@@ -291,12 +290,92 @@
     to_before.start()
     to_after.start()
     physics(2, chunks)
+
+    rows_here = cells // LANES
+    streams = 3
+    bands = levels // (8 * streams)
+    center, scale = viscosity(section)
+
+    def level(low, s):
+        return pl.ds(low + 8 * s if isinstance(low, int) else pl.multiple_of(low + 8 * s, 8), 8)
+
+    def here(low, row):
+        return [x_v[level(low, s), pl.ds(row * LANES, LANES)] for s in range(streams)]
+
+    def keep(low, row, values):
+        for s in range(streams):
+            p_v[level(low, s), pl.ds((row + HALF) * LANES, LANES)] = values[s] * scale
+
+    def inner(band):
+        inside = pl.ds(2 * HALF * LANES, (rows_here - 2 * HALF) * LANES)
+        span = pl.ds(pl.multiple_of(band * 8 * streams, 8), 8 * streams)
+        return pltpu.make_async_copy(p_v.at[span, inside], out_hbm.at[span, inside], store_sem.at[band])
+
+    def interior(band, carry):
+        low = band * 8 * streams
+        march(
+            rows_here,
+            16,
+            streams,
+            functools.partial(here, low),
+            lambda row, values: keep(low, row - HALF, values),
+            lambda row: None,
+            coef_v,
+            center,
+        )
+        inner(band).start()
+        return carry
+
+    lax.fori_loop(0, bands, interior, 0)
+
+    for copy in (to_before, to_after):
+        copy.wait()
+    top = jnp.where(me == 0, 0.0, 1.0).astype(jnp.float32)
+    bottom = jnp.where(me == peers - 1, 0.0, 1.0).astype(jnp.float32)
+    edge_rows = 2 * STEPS
+    for band in range(bands):
+        low = band * 8 * streams
+
+        def upper(row, low=low):
+            if row >= STEPS:
+                return here(low, row - STEPS)
+            return [north_v[level(low, s), pl.ds(row * LANES, LANES)] for s in range(streams)]
+
+        def lower(row, low=low):
+            if row < STEPS:
+                return here(low, rows_here - STEPS + row)
+            return [south_v[level(low, s), pl.ds((row - STEPS) * LANES, LANES)] for s in range(streams)]
+
+        march(
+            edge_rows,
+            edge_rows,
+            streams,
+            upper,
+            lambda row, values, low=low: keep(low, row - STEPS - HALF, values),
+            lambda row: top if row < STEPS else None,
+            coef_v,
+            center,
+        )
+        march(
+            edge_rows,
+            edge_rows,
+            streams,
+            lower,
+            lambda row, values, low=low: keep(low, rows_here - STEPS + row - HALF, values),
+            lambda row: bottom if row >= STEPS else None,
+            coef_v,
+            center,
+        )
+    stores = [inner(band) for band in range(bands)]
+    for number, begin in enumerate((0, rows_here * LANES)):
+        ends = pl.ds(begin, 2 * HALF * LANES)
+        store = pltpu.make_async_copy(p_v.at[:, ends], out_hbm.at[:, ends], store_sem.at[bands + number])
+        store.start()
+        stores.append(store)
     for copy in data + meta:
         copy.wait_send()
-    for i in range(chunks):
-        put(i).wait()
-    for copy in (to_before, to_after):
-        copy.wait()
+    for store in stores:
+        store.wait()
 
 
 def ring_powers():
@@ -305,7 +384,7 @@
         lax.broadcasted_iota(jnp.int32, shape, 0) + 2 * LANES - lax.broadcasted_iota(jnp.int32, shape, 1)
     ) % LANES
     terms = []
-    for entries in ({1: 4}, {0: 12, 2: 6}, {1: 12, 3: 4}, {0: 6, 2: 4, 4: 1}):
+    for entries in ({1: 2}, {0: 2, 2: 1}):
         term = jnp.zeros(shape, jnp.float32)
         for distance, weight in entries.items():
             near = (apart == distance) | (apart == (LANES - distance) % LANES)
@@ -314,100 +393,96 @@
     return jnp.concatenate(terms, axis=1)
 
 
-def diffuse(x_ref, north_ref, south_ref, o_ref, coef_ref, side_ref):
-    levels, cells = x_ref.shape
-    rows = cells // LANES
-    streams = levels // 8
-    chunk = 32
-    first = 2 * STEPS
-    section = lax.axis_index("sec")
-    me = lax.axis_index("tile")
-    peers = lax.axis_size("tile")
+def viscosity(section):
     visc = jnp.where(section == 0, ATMOS_VISC, OCEAN_VISC).astype(jnp.float32)
-    center = (1.0 - 4.0 * visc) / visc
-    scale = (visc * visc) * (visc * visc)
-    top = jnp.where(me == 0, 0.0, 1.0).astype(jnp.float32)
-    bottom = jnp.where(me == peers - 1, 0.0, 1.0).astype(jnp.float32)
-
-    @pl.when(pl.program_id(0) == 0)
-    def _():
-        coef_ref[...] = ring_powers()
-
-    coef = coef_ref[...]
-
-    def at(row):
-        return row * LANES if isinstance(row, int) else pl.multiple_of(row * LANES, LANES)
-
-    def load(ref, row):
-        return [ref[pl.ds(8 * s, 8), pl.ds(at(row), LANES)] for s in range(streams)]
-
-    def store(row, values):
-        for s in range(streams):
-            o_ref[0, pl.ds(8 * s, 8), pl.ds(at(row), LANES)] = values[s] * scale
-
-    def sides(ref, row, count, place):
-        value = jnp.concatenate([v for i in range(count) for v in load(ref, row + i)], axis=0)
+    return (1.0 - 4.0 * visc) / visc, visc * visc
+
+
+def march(total, chunk, streams, load, emit, mask, coef_ref, center):
+    def sides(row):
+        value = jnp.concatenate([v for i in range(chunk) for v in load(row + i)], axis=0)
         high = value.astype(jnp.bfloat16)
         low = (value - high.astype(jnp.float32)).astype(jnp.bfloat16)
-        terms = jnp.dot(
-            jnp.concatenate([high, low], axis=1), coef, preferred_element_type=jnp.float32
-        )
-        for i in range(count):
+        return jnp.dot(
+            jnp.concatenate([high, low], axis=1), coef_ref[...], preferred_element_type=jnp.float32
+        )
+
+    zero = jnp.zeros((8, LANES), jnp.float32)
+    carry = [[(zero, zero) for _ in range(HALF)] for _ in range(streams)]
+    late = [zero] * streams
+    terms = sides(0)
+    for begin in range(0, total, chunk):
+        ahead = sides(begin + chunk) if begin + chunk < total else None
+        for i in range(chunk):
+            row = begin + i
+            new = load(row)
+            values = []
             for s in range(streams):
                 m = (i * streams + s) * 8
-                for k in range(STEPS):
-                    side_ref[place + i, s, k] = terms[m : m + 8, k * LANES : (k + 1) * LANES]
-
-    def advance(new, carry, row, edges):
-        values, kept = [], []
-        for s in range(streams):
-            value, parts = new[s], []
-            for k in range(STEPS):
-                part, prior = carry[s][k]
-                if edges and row - k < 0:
-                    value = value * top
-                if edges and row - k >= rows:
-                    value = value * bottom
-                parts.append((center * value + (side_ref[first + row - k, s, k] + prior), value))
-                value = part + value
-            values.append(value)
-            kept.append(tuple(parts))
-        return values, tuple(kept)
-
-    zero = jnp.zeros((8, LANES), jnp.float32)
-    carry = tuple(tuple((zero, zero) for _ in range(STEPS)) for _ in range(streams))
-    for row in range(STEPS):
-        for s in range(streams):
-            for k in range(STEPS):
-                side_ref[row, s, k] = zero
-    sides(north_ref, 0, STEPS, first - STEPS)
-    sides(x_ref, 0, chunk, first)
-    for row in range(-STEPS, 0):
-        _, carry = advance(load(north_ref, row + STEPS), carry, row, True)
-
-    def several(i, carry, start=0, edges=False):
-        for u in range(start, chunk):
-            row = i * chunk + u
-            values, carry = advance(load(x_ref, row), carry, row, edges)
-            store(row - STEPS, values)
+                now = (terms[m : m + 8, :LANES], late[s])
+                late[s] = terms[m : m + 8, LANES:]
+                value = new[s]
+                for k in range(HALF):
+                    part, prior = carry[s][k]
+                    factor = mask(row - k)
+                    if factor is not None:
+                        value = value * factor
+                    carry[s][k] = (center * value + (now[k] + prior), value)
+                    value = part + value
+                values.append(value)
+            if row >= 2 * HALF:
+                emit(row, values)
+        terms = ahead
+
+
+def diffuse(x_hbm, o_hbm, x_v, o_v, coef_ref, get_sem, put_sem):
+    levels, cells = x_v.shape
+    rows = cells // LANES
+    streams = 3
+    bands = levels // (8 * streams)
+    center, scale = viscosity(lax.axis_index("sec"))
+    me = lax.axis_index("tile")
+    top = jnp.where(me == 0, 0.0, 1.0).astype(jnp.float32)
+    bottom = jnp.where(me == lax.axis_size("tile") - 1, 0.0, 1.0).astype(jnp.float32)
+
+    def span(band):
+        low = band * 8 * streams
+        return pl.ds(low if isinstance(band, int) else pl.multiple_of(low, 8), 8 * streams)
+
+    def get(band):
+        return pltpu.make_async_copy(x_hbm.at[span(band)], x_v.at[span(band)], get_sem.at[band])
+
+    def put(band):
+        return pltpu.make_async_copy(o_v.at[span(band)], o_hbm.at[0, span(band)], put_sem.at[band])
+
+    for band in range(bands):
+        get(band).start()
+    coef_ref[...] = ring_powers()
+
+    def part(band, carry):
+        low = band * 8 * streams
+
+        def level(s):
+            return pl.ds(pl.multiple_of(low + 8 * s, 8), 8)
+
+        def load(row):
+            return [x_v[level(s), pl.ds(row * LANES, LANES)] for s in range(streams)]
+
+        def emit(row, values):
+            for s in range(streams):
+                o_v[level(s), pl.ds((row - 2 * HALF) * LANES, LANES)] = values[s] * scale
+
+        def mask(row):
+            return top if row < HALF else (bottom if row >= rows - HALF else None)
+
+        get(band).wait()
+        march(rows, 12, streams, load, emit, mask, coef_ref, center)
+        put(band).start()
         return carry
 
-    for row in range(STEPS):
-        _, carry = advance(load(x_ref, row), carry, row, True)
-    sides(x_ref, chunk, chunk, first + chunk)
-    carry = several(0, carry, STEPS)
-
-    def body(i, carry):
-        sides(x_ref, (i + 1) * chunk, chunk, first + (i + 1) * chunk)
-        return several(i, carry)
-
-    last = rows // chunk - 1
-    carry = lax.fori_loop(1, last, body, carry)
-    sides(south_ref, 0, STEPS, first + rows)
-    carry = several(last, carry)
-    for row in range(rows, rows + STEPS):
-        values, carry = advance(load(south_ref, row - rows), carry, row, True)
-        store(row - STEPS, values)
+    lax.fori_loop(0, bands, part, 0)
+    for band in range(bands):
+        put(band).wait()
 
 
 def per_device(dims, section_state, matrices, blocks, src_slot, dst_dev, dst_slot):
@@ -416,19 +491,16 @@
     tiles = cells // LANES
     peers = dims[0] * dims[1] * dims[2]
     halo = STEPS * LANES
+    wide = cells + 2 * HALF * LANES
     f32, i32, dma = jnp.float32, jnp.int32, pltpu.SemaphoreType.DMA
     anywhere = pl.BlockSpec(memory_space=pl.ANY)
     vmem = pl.BlockSpec(memory_space=pltpu.VMEM)
     slots = peers * DEPTH * FIELDS
-    state, north, south = pl.pallas_call(
+    state = pl.pallas_call(
         functools.partial(exchange, dims),
-        out_shape=[
-            jax.ShapeDtypeStruct((levels, cells), f32),
-            jax.ShapeDtypeStruct((levels, halo), f32),
-            jax.ShapeDtypeStruct((levels, halo), f32),
-        ],
+        out_shape=jax.ShapeDtypeStruct((levels, wide), f32),
         in_specs=[anywhere, vmem, anywhere, pl.BlockSpec(memory_space=pltpu.SMEM), vmem, vmem],
-        out_specs=[anywhere, anywhere, anywhere],
+        out_specs=anywhere,
         scratch_shapes=[
             pltpu.VMEM((block_count, LANES, LANES), jnp.bfloat16),
             pltpu.VMEM((FIELDS, cells), f32),
@@ -439,8 +511,11 @@
             pltpu.VMEM((peers, 1, LANES), f32),
             pltpu.VMEM((peers, 1, LANES), f32),
             pltpu.VMEM((levels, cells), f32),
-            pltpu.VMEM((levels, cells), f32),
+            pltpu.VMEM((levels, wide), f32),
             pltpu.VMEM((tiles * FIELDS, LANES), f32),
+            pltpu.VMEM((levels, halo), f32),
+            pltpu.VMEM((levels, halo), f32),
+            pltpu.VMEM((2 * LANES, HALF * LANES), jnp.bfloat16),
             pltpu.VMEM((8, peers * DEPTH), i32),
             pltpu.SMEM((8, peers * DEPTH), i32),
             dma((10,)),
@@ -464,23 +539,20 @@
         dst_dev.reshape(1, block_count),
         dst_slot,
     )
-    band = 24
     return pl.pallas_call(
         diffuse,
-        grid=(levels // band,),
         out_shape=jax.ShapeDtypeStruct((1, levels, cells), f32),
-        in_specs=[
-            pl.BlockSpec((band, cells), lambda i: (i, 0)),
-            pl.BlockSpec((band, halo), lambda i: (i, 0)),
-            pl.BlockSpec((band, halo), lambda i: (i, 0)),
-        ],
-        out_specs=pl.BlockSpec((1, band, cells), lambda i: (0, i, 0)),
+        in_specs=[anywhere],
+        out_specs=anywhere,
         scratch_shapes=[
-            pltpu.VMEM((2 * LANES, STEPS * LANES), jnp.bfloat16),
-            pltpu.VMEM((cells // LANES + 3 * STEPS, band // 8, STEPS, 8, LANES), f32),
+            pltpu.VMEM((levels, wide), f32),
+            pltpu.VMEM((levels, cells), f32),
+            pltpu.VMEM((2 * LANES, HALF * LANES), jnp.bfloat16),
+            dma((8,)),
+            dma((8,)),
         ],
         compiler_params=pltpu.CompilerParams(vmem_limit_bytes=VMEM_BYTES),
-    )(state, north, south)
+    )(state)
 
 
 def solution(mesh):

time: 58.4 us -> 55.1 us (0.943)
  Pallas kernels: 58.2 us -> 54.9 us
    pallas_call x2, Pallas kernels: 58.2 us -> 54.9 us  [the longest x1 49.8 us: per_device(): pl.pallas_call(functools.partial(exchange, dims), out_shape=jax.ShapeDtyp...]
where the time goes in v2:
time: 55.1 us; the launch traced here: 54.9 us
  Pallas kernels  54.9 us (100%)
    pallas_call x1, Pallas kernels, per_device(): pl.pallas_call(functools.partial(exchange, dims), out_shape=jax.ShapeDtyp...  49.8 us
    pallas_call x1, Pallas kernels, per_device(): pl.pallas_call(diffuse, out_shape=jax.ShapeDtypeStruct((1, levels, cells)...  5.12 us

profile of v2, /device:TPU:0, one launch (start us, length us, event | category | flops | bytes accessed | tf_op | source)
XLA Modules:
  0.0 54.9 jit_solution(9513857819670622757)
XLA Ops:
  0.0 49.8 %shard_map.64.x_hbm = f32[72,16896]{1,0:T(8,128)} custom-call(f32[72,16384]{1,0:T(8,128)} %bitcast.4, f32[2,72,72]{2,1,0:T(8,128)} %mats.1, bf16[256,128,128]{2,1,0:T(8,128)(2,1)} %bitcast.3, s32[1,256]{1,0:T(1,128)} %src_slot.1, s32[1,256]{1,0:T(1,128)} %bitcast.5, s32[1,256]{1,0:T(1,128)} %dst_slot.1), custom_call_target="tpu_custom_call" | custom-call | tf_op jit(solution)/shard_map/pallas_call | solution.py:499
  49.8 5.1 %shard_map.65 = f32[1,72,16384]{2,1,0:T(8,128)} custom-call(f32[72,16896]{1,0:T(8,128)} %shard_map.64.x_hbm), custom_call_target="tpu_custom_call" | custom-call | tf_op jit(solution)/shard_map/pallas_call | solution.py:542

commit v3 on v2

--- a/solution.py
+++ b/solution.py
@@ -99,13 +99,15 @@
     other = 1 - section
     y, x, z = me // (dims[1] * dims[2]), (me // dims[2]) % dims[1], me % dims[2]
 
+    turn = 1 - 2 * section
+
     def at(offset, sign):
-        dy, dx, dz = offset
+        dy, dx, dz = [sign * turn * a for a in offset]
         ny, nx, nz = dims
         return (
-            ((y + ny + sign * dy) % ny) * (nx * nz)
-            + ((x + nx + sign * dx) % nx) * nz
-            + (z + nz + sign * dz) % nz
+            ((y + ny + dy) % ny) * (nx * nz)
+            + ((x + nx + dx) % nx) * nz
+            + (z + nz + dz) % nz
         )
 
     after, before = (me + 1) % peers, (me + peers - 1) % peers
@@ -125,7 +127,7 @@
 
     barrier = pltpu.get_barrier_semaphore()
     for offset in order:
-        pl.semaphore_signal(barrier, inc=1, device_id=(other, at(offset, -1)), device_id_type=MESH)
+        pl.semaphore_signal(barrier, inc=1, device_id=(other, at(offset, 1)), device_id_type=MESH)
     for side in (before, after):
         pl.semaphore_signal(barrier, inc=1, device_id=(section, side), device_id_type=MESH)
 
@@ -239,38 +241,39 @@
             else:
                 imp_v[to, :] = imp_v[to, :] + term
 
-    width = 2048
-    chunks = cells // width
-    per_width = width // LANES
-
-    def columns(substeps, i, carry):
-        i = (i + chunks - 1) % chunks
-        cols = pl.ds(pl.multiple_of(i * width, width), width)
+    halo = STEPS * LANES
+    width = 1536
+
+    def rows_of(tile):
+        return pl.ds(tile * FIELDS if isinstance(tile, int) else pl.multiple_of(tile * FIELDS, FIELDS), FIELDS)
+
+    def columns(substeps, low, width):
+        first = low // LANES
+        if not isinstance(low, int):
+            low = pl.multiple_of(low, LANES)
+        cols = pl.ds(low, width)
         imported = jnp.concatenate(
-            [
-                imp_v[pl.ds(pl.multiple_of((i * per_width + j) * FIELDS, FIELDS), FIELDS), :]
-                for j in range(per_width)
-            ],
-            axis=1,
-        )
-        x_v[pl.ds(start, FIELDS), cols] = x_v[pl.ds(start, FIELDS), cols] + imported
+            [imp_v[rows_of(first + j), :] for j in range(width // LANES)], axis=1
+        )
+        value = x_v[:, cols]
+        if substeps == 2:
+            value = jnp.concatenate([value[:-FIELDS], value[-FIELDS:] + imported], axis=0)
+        else:
+            value = jnp.concatenate([value[:FIELDS] + imported, value[FIELDS:]], axis=0)
         product = p_v[:, cols] + jnp.dot(edge, stacked(imported), preferred_element_type=jnp.float32)
-        value = x_v[:, cols] + 0.5 * jnp.tanh(product)
+        value = value + 0.5 * jnp.tanh(product)
         if substeps == 2:
             product = jnp.dot(full, stacked(value), preferred_element_type=jnp.float32)
             value = value + 0.5 * jnp.tanh(product)
         x_v[:, cols] = value
-        return carry
-
-    def physics(low, high):
-        for number in range(2):
-
-            @pl.when(section == number)
-            def _(number=number):
-                lax.fori_loop(low, high, functools.partial(columns, 2 - number), 0)
-
-    physics(0, 2)
-    halo = STEPS * LANES
+
+    for number in range(2):
+
+        @pl.when(section == number)
+        def _(number=number):
+            columns(2 - number, 0, halo)
+            columns(2 - number, cells - halo, halo)
+
     to_before = pltpu.make_async_remote_copy(
         src_ref=x_v.at[:, pl.ds(0, halo)],
         dst_ref=south_v,
@@ -289,7 +292,16 @@
     )
     to_before.start()
     to_after.start()
-    physics(2, chunks)
+
+    def middle(substeps, i, carry):
+        columns(substeps, halo + i * width, width)
+        return carry
+
+    for number in range(2):
+
+        @pl.when(section == number)
+        def _(number=number):
+            lax.fori_loop(0, (cells - 2 * halo) // width, functools.partial(middle, 2 - number), 0)
 
     rows_here = cells // LANES
     streams = 3

time: 55.1 us -> 53.9 us (0.978)
  Pallas kernels: 54.9 us -> 53.7 us
    pallas_call x1, Pallas kernels: 49.8 us -> 48.6 us  [per_device(): pl.pallas_call(functools.partial(exchange, dims), out_shape=jax.ShapeDtyp...]
where the time goes in v3:
time: 53.9 us; the launch traced here: 53.7 us
  Pallas kernels  53.7 us (100%)
    pallas_call x1, Pallas kernels, per_device(): pl.pallas_call(functools.partial(exchange, dims), out_shape=jax.ShapeDtyp...  48.6 us
    pallas_call x1, Pallas kernels, per_device(): pl.pallas_call(diffuse, out_shape=jax.ShapeDtypeStruct((1, levels, cells)...  5.12 us

profile of v3, /device:TPU:0, one launch (start us, length us, event | category | flops | bytes accessed | tf_op | source)
XLA Modules:
  0.0 53.7 jit_solution(3033088098068906306)
XLA Ops:
  0.0 48.6 %shard_map.64.x_hbm = f32[72,16896]{1,0:T(8,128)} custom-call(f32[72,16384]{1,0:T(8,128)} %bitcast.4, f32[2,72,72]{2,1,0:T(8,128)} %mats.1, bf16[256,128,128]{2,1,0:T(8,128)(2,1)} %bitcast.3, s32[1,256]{1,0:T(1,128)} %src_slot.1, s32[1,256]{1,0:T(1,128)} %bitcast.5, s32[1,256]{1,0:T(1,128)} %dst_slot.1), custom_call_target="tpu_custom_call" | custom-call | tf_op jit(solution)/shard_map/pallas_call | solution.py:511
  48.6 5.1 %shard_map.65 = f32[1,72,16384]{2,1,0:T(8,128)} custom-call(f32[72,16896]{1,0:T(8,128)} %shard_map.64.x_hbm), custom_call_target="tpu_custom_call" | custom-call | tf_op jit(solution)/shard_map/pallas_call | solution.py:554

commit v4 on v3

--- a/solution.py
+++ b/solution.py
@@ -32,7 +32,7 @@
     def hops(offset):
         return sum(min(a, n - a) for a, n in zip(offset, dims))
 
-    return sorted(offsets, key=lambda offset: -hops(offset))
+    return sorted(offsets, key=lambda offset: -hops(offset) - 0.5 * min(offset[2], dims[2] - offset[2]))
 
 
 def split(value):

time: 53.9 us -> 55.9 us (1.037)
  Pallas kernels: 53.7 us -> 55.8 us
    pallas_call x1, Pallas kernels: 48.6 us -> 50.7 us  [per_device(): pl.pallas_call(functools.partial(exchange, dims), out_shape=jax.ShapeDtyp...]
where the time goes in v4:
time: 55.9 us; the launch traced here: 55.8 us
  Pallas kernels  55.8 us (100%)
    pallas_call x1, Pallas kernels, per_device(): pl.pallas_call(functools.partial(exchange, dims), out_shape=jax.ShapeDtyp...  50.7 us
    pallas_call x1, Pallas kernels, per_device(): pl.pallas_call(diffuse, out_shape=jax.ShapeDtypeStruct((1, levels, cells)...  5.12 us

profile of v4, /device:TPU:0, one launch (start us, length us, event | category | flops | bytes accessed | tf_op | source)
XLA Modules:
  0.0 55.8 jit_solution(3358159639107639784)
XLA Ops:
  0.0 50.7 %shard_map.64.x_hbm = f32[72,16896]{1,0:T(8,128)} custom-call(f32[72,16384]{1,0:T(8,128)} %bitcast.4, f32[2,72,72]{2,1,0:T(8,128)} %mats.1, bf16[256,128,128]{2,1,0:T(8,128)(2,1)} %bitcast.3, s32[1,256]{1,0:T(1,128)} %src_slot.1, s32[1,256]{1,0:T(1,128)} %bitcast.5, s32[1,256]{1,0:T(1,128)} %dst_slot.1), custom_call_target="tpu_custom_call" | custom-call | tf_op jit(solution)/shard_map/pallas_call | solution.py:511
  50.7 5.1 %shard_map.65 = f32[1,72,16384]{2,1,0:T(8,128)} custom-call(f32[72,16896]{1,0:T(8,128)} %shard_map.64.x_hbm), custom_call_target="tpu_custom_call" | custom-call | tf_op jit(solution)/shard_map/pallas_call | solution.py:554
